TPU v7x, 32 devices: a whole 2x2x4 slice. The times are simulated.
32 devices in a mesh: wide: 8 (over z, x), tensor: 4 (over y, core).
Axes of the slice: x: 2, y: 2, z: 4, core: 2. Of those that a mesh axis runs over, the one named last changes fastest.
Arguments:
- tokens: bfloat16 [4096, 8192], P('wide', 'tensor'), may hold values from -6 to 6
- key_value_weight: bfloat16 [8192, 2048], P(None, 'tensor'), may hold values from -0.0625 to 0.0625
- adapter_down_maps: bfloat16 [8192, 128, 64], P('tensor', 'wide'), may hold values from -0.0625 to 0.0625
- adapter_up_maps: bfloat16 [128, 64, 2048], P('wide', None, 'tensor'), may hold values from -0.75 to 0.75
- adapter_per_row: int32 [4096], P('wide'), may hold values from 0 to 127, as said below
- adapter_storage_slot: int32 [128], replicated, may hold values from 0 to 127, as said below
Outputs:
- kv_out: bfloat16 [4096, 2048], P('wide', 'tensor')
Inputs may be any that keep to these rules, and one draw needn't show every extreme that they name: `adapter_per_row`: the adapter stored at position p belongs to owner p // 16 of wide. Among the 512 rows of one index of wide, at most 128 name adapters of one owner; in every draw one owner gets exactly 128 rows from every index of wide. `adapter_storage_slot`: each position is taken by exactly one adapter.
All inputs are finite; a program needn't handle non-finite values.
Results may differ from a plain program's by a relative error of at most 0.0049.
Values may be sent and summed in bfloat16 or wider, within the bound.
A program may use at most 64 MiB of HBM per device.

v0:
```python
import jax
import jax.numpy as jnp
from jax import lax
from jax.sharding import PartitionSpec as P


def body(
    tokens,
    key_value_weight,
    adapter_down_maps,
    adapter_up_maps,
    adapter_per_row,
    adapter_storage_slot,
):
    row_count = tokens.shape[0]
    feature_portion = tokens.shape[1]
    wide_count = lax.axis_size("wide")
    capacity = 2 * row_count // wide_count
    present_adapters = adapter_down_maps.shape[1]
    rank_dimension = adapter_down_maps.shape[2]
    column_portion = key_value_weight.shape[1]
    gathered = lax.all_gather(tokens, "tensor", axis=1, tiled=True)
    base_projection_output = jnp.dot(gathered, key_value_weight, preferred_element_type=jnp.float32)
    total_adapters = adapter_storage_slot.shape[0]
    adapter_match = adapter_per_row[:, None] == jnp.arange(total_adapters, dtype=jnp.int32)[None, :]
    storage_position = jnp.sum(jnp.where(adapter_match, adapter_storage_slot[None, :], 0), axis=1)
    owner_index = storage_position // present_adapters
    local_index = storage_position % present_adapters
    owner_onehot = (
        owner_index[:, None] == jnp.arange(wide_count, dtype=jnp.int32)[None, :]
    ).astype(jnp.int32)
    earlier = jnp.cumsum(owner_onehot, axis=0) - owner_onehot
    rank_in_owner = jnp.sum(earlier * owner_onehot, axis=1)
    storage_slot_index = owner_index * capacity + rank_in_owner
    send_rows = (
        jnp.zeros((wide_count * capacity, feature_portion), jnp.bfloat16)
        .at[storage_slot_index]
        .set(tokens)
    )
    send_slots = (
        jnp.full((wide_count * capacity,), -1, jnp.int32).at[storage_slot_index].set(local_index)
    )
    send_rows = send_rows.reshape(wide_count, capacity, feature_portion)
    send_slots = send_slots.reshape(wide_count, capacity)
    down_matrix = adapter_down_maps.reshape(feature_portion, present_adapters * rank_dimension)
    up_matrix = adapter_up_maps.reshape(present_adapters * rank_dimension, column_portion)
    column_adapter = (
        jnp.arange(present_adapters * rank_dimension, dtype=jnp.int32) // rank_dimension
    )
    got_rows = lax.all_to_all(send_rows, "wide", split_axis=0, concat_axis=0, tiled=True)
    got_slots = lax.all_to_all(send_slots, "wide", split_axis=0, concat_axis=0, tiled=True)
    source_rows, entry_list = got_slots.shape
    flat_rows = got_rows.reshape(source_rows * entry_list, feature_portion)
    slot_adapter = got_slots.reshape(source_rows * entry_list)
    all_ranks = jnp.dot(flat_rows, down_matrix, preferred_element_type=jnp.float32)
    selected = slot_adapter[:, None] == column_adapter[None, :]
    partial_value = jnp.sum(
        jnp.where(selected, all_ranks, 0.0).reshape(
            source_rows * entry_list, present_adapters, rank_dimension
        ),
        axis=1,
    )
    summed = lax.psum(partial_value, "tensor")
    reduced_rows = summed.astype(jnp.bfloat16)
    expanded_rows = jnp.where(
        selected, jnp.tile(reduced_rows, (1, present_adapters)), jnp.zeros((), jnp.bfloat16)
    )
    adapter_correction = jnp.dot(
        expanded_rows, up_matrix, preferred_element_type=jnp.float32
    ).astype(jnp.bfloat16)
    adapter_correction = adapter_correction.reshape(source_rows, entry_list, column_portion)
    returned_rows = lax.all_to_all(
        adapter_correction, "wide", split_axis=0, concat_axis=0, tiled=True
    )
    returned_rows = returned_rows.reshape(wide_count * capacity, column_portion)
    adapter_row_output = returned_rows[storage_slot_index]
    return (base_projection_output + adapter_row_output.astype(jnp.float32)).astype(jnp.bfloat16)


def solution(mesh):
    in_specs = (
        P("wide", "tensor"),
        P(None, "tensor"),
        P("tensor", "wide", None),
        P("wide", None, "tensor"),
        P("wide"),
        P(),
    )
    out_specs = P("wide", "tensor")
    return jax.shard_map(body, mesh=mesh, in_specs=in_specs, out_specs=out_specs, check_vma=False)
```

profile of v0, /device:TPU:0, one launch (start us, length us, event | category | flops | bytes accessed | tf_op | source)
XLA Modules:
  0.0 204.7 jit_solution(3429088262360880170)
XLA Ops:
  6.5 0.0 copy-start
  6.5 0.0 all-gather.2.cloned.1.call-start
  6.5 0.7 all-gather.2.cloned.1.call-update
  7.3 0.9 select_reduce_fusion
  8.2 1.1 reduce-window.6
  9.4 0.2 slice_reduce_fusion
  9.6 0.1 fusion.9
  9.8 3.0 %scatter_custom_fusion = s32[1024]{0:T(1024)} fusion(s32[512]{0:T(512)S(1)} %bitcast.46, s32[512]{0:T(512)S(1)} %get-tuple-element.5, s32[]{:T(128)} %constant.50.clone.1), kind=kCustom, calls=%fused_computation.56 | custom fusion | bytes 4100 | tf_op jit(solution)/shard_map/scatter | solution.py:41
  12.8 7.3 %all-to-all-start = ((s32[8,1,128]{2,1,0:T(1,128)}), s32[8,1,128]{2,1,0:T(1,128)S(1)}, u32[]{:S(2)}, u32[]{:S(2)}) async-start(s32[8,1,128]{2,1,0:T(1,128)} %bitcast.6), calls=%async_computation | async-start | bytes 8192 | tf_op jit(solution)/shard_map/all_to_all | solution.py:51
  20.0 7.5 %scatter_custom_fusion.1 = bf16[1024,2048]{1,0:T(8,128)(2,1)} fusion(s32[512]{0:T(512)S(1)} %bitcast.47, bf16[512,2048]{1,0:T(8,128)(2,1)} %param.6, bf16[]{:T(256)} %constant.61.clone.1), kind=kCustom, calls=%fused_computation.7 | custom fusion | bytes 4194816 | tf_op jit(solution)/shard_map/scatter | solution.py:38
  27.5 0.0 all-to-all-done
  27.5 5.9 %all-to-all-start.1 = ((bf16[8,128,2048]{2,1,0:T(8,128)(2,1)}), bf16[8,128,2048]{2,1,0:T(8,128)(2,1)}, u32[]{:S(2)}, u32[]{:S(2)}) async-start(bf16[8,128,2048]{2,1,0:T(8,128)(2,1)} %bitcast.43), calls=%async_computation.1 | async-start | bytes 8388608 | tf_op jit(solution)/shard_map/all_to_all | solution.py:50
  33.5 92.8 %all-to-all-done.1 = bf16[8,128,2048]{2,1,0:T(8,128)(2,1)} async-done(((bf16[8,128,2048]{2,1,0:T(8,128)(2,1)}), bf16[8,128,2048]{2,1,0:T(8,128)(2,1)}, u32[]{:S(2)}, u32[]{:S(2)}) %all-to-all-start.1) | async-done | bytes 4194336 | tf_op jit(solution)/shard_map/all_to_all | solution.py:50
  126.3 10.0 %compare_select_fusion = f32[1024,1024]{0,1:T(8,128)} fusion(s32[1024]{0:T(1024)S(1)} %bitcast.50, s32[1024]{0:T(1024)S(1)} %add_select_fusion.1, bf16[1024,2048]{1,0:T(8,128)(2,1)} %bitcast.9, bf16[2048,1024]{0,1:T(8,128)(2,1)} %bitcast.52), kind=kOutput, calls=%fused_computation.3 | convolution fusion | flops 4297064448 | bytes 12591104 | tf_op jit(solution)/shard_map/dot_general | solution.py:55
  136.2 2.5 %reduce_sum.38 = f32[1024,64]{0,1:T(8,128)S(1)} reduce(f32[1024,16,64]{0,2,1:T(8,128)} %bitcast.44, f32[]{:T(128)} %constant.62.clone.1), dimensions={1}, to_apply=%region_6.7 | reduce | flops 983040 | bytes 4456452 | tf_op jit(solution)/shard_map/reduce_sum | solution.py:57
  138.7 13.2 %all-reduce.1 = bf16[1024,64]{0,1:T(8,128)(2,1)S(1)} all-reduce(f32[1024,64]{0,1:T(8,128)S(1)} %reduce_sum.38), channel_id=1, replica_groups=mesh['wide'=8,'tensor'=4] {'tensor'}, use_global_device_ids=true, to_apply=%region_7.8 | all-reduce | flops 65536 | bytes 393216 | tf_op jit(solution)/shard_map/psum | solution.py:63
  151.9 0.0 copy-done
  151.9 2.5 %bitcast_convert_fusion = bf16[1024,512]{1,0:T(8,128)(2,1)} fusion(bf16[16,64,512]{2,1,0:T(8,128)(2,1)S(1)} %copy-done, s32[16,64]{1,0:T(8,128)S(1)} %add_select_fusion, s32[1024]{0:T(1024)S(1)} %bitcast.51, bf16[1024,64]{0,1:T(8,128)(2,1)S(1)} %all-reduce.1), kind=kOutput, calls=%fused_computation.6 | convolution fusion | flops 1076363264 | bytes 2236416 | tf_op jit(solution)/shard_map/dot_general | solution.py:68
  154.4 5.3 %all-to-all-start.2 = ((bf16[8,128,512]{2,1,0:T(8,128)(2,1)}), bf16[8,128,512]{2,1,0:T(8,128)(2,1)S(1)}, u32[]{:S(2)}, u32[]{:S(2)}) async-start(bf16[8,128,512]{2,1,0:T(8,128)(2,1)} %bitcast.13), calls=%async_computation.2 | async-start | bytes 2097152 | tf_op jit(solution)/shard_map/all_to_all | solution.py:72
  159.7 25.2 %all-to-all-done.2 = bf16[8,128,512]{2,1,0:T(8,128)(2,1)S(1)} async-done(((bf16[8,128,512]{2,1,0:T(8,128)(2,1)}), bf16[8,128,512]{2,1,0:T(8,128)(2,1)S(1)}, u32[]{:S(2)}, u32[]{:S(2)}) %all-to-all-start.2) | async-done | bytes 1048608 | tf_op jit(solution)/shard_map/all_to_all | solution.py:72
  184.8 2.0 gather_fusion
  186.8 0.0 all-gather.2.cloned.1.call-done
  186.8 11.0 %fusion.5 = bf16[512,512]{1,0:T(8,128)(2,1)} fusion(bf16[512,8192]{1,0:T(8,128)(2,1)} %all-gather.2.cloned.1.call-done, bf16[8192,512]{1,0:T(8,128)(2,1)} %param.7, bf16[512,512]{1,0:T(8,128)(2,1)S(1)} %gather_fusion), kind=kOutput, calls=%fused_computation.12 | convolution fusion | flops 4295753728 | bytes 17825792 | tf_op jit(solution)/shard_map/dot_general | solution.py:23
  (9 shorter events, 0.1 us)
Async XLA Ops:
  6.5 145.4 %copy-start = (bf16[16,64,512]{2,1,0:T(8,128)(2,1)S(1)}, bf16[16,64,512]{2,1,0:T(8,128)(2,1)}, u32[]{:S(2)}) copy-start(bf16[16,64,512]{2,1,0:T(8,128)(2,1)} %param.9) | copy-start | bytes 3145732
  6.5 180.3 %all-gather.2.cloned.1.call-start = ((), (), s32[]{:S(2)}) async-start(), calls=%async_computation.3 | async-start | bytes 10485760 | tf_op jit(solution)/shard_map/all_gather | solution.py:22
  12.8 14.8 %all-to-all-start = ((s32[8,1,128]{2,1,0:T(1,128)}), s32[8,1,128]{2,1,0:T(1,128)S(1)}, u32[]{:S(2)}, u32[]{:S(2)}) async-start(s32[8,1,128]{2,1,0:T(1,128)} %bitcast.6), calls=%async_computation | async-start | bytes 8192 | tf_op jit(solution)/shard_map/all_to_all | solution.py:51
  27.5 98.8 %all-to-all-start.1 = ((bf16[8,128,2048]{2,1,0:T(8,128)(2,1)}), bf16[8,128,2048]{2,1,0:T(8,128)(2,1)}, u32[]{:S(2)}, u32[]{:S(2)}) async-start(bf16[8,128,2048]{2,1,0:T(8,128)(2,1)} %bitcast.43), calls=%async_computation.1 | async-start | bytes 8388608 | tf_op jit(solution)/shard_map/all_to_all | solution.py:50
  154.4 30.4 %all-to-all-start.2 = ((bf16[8,128,512]{2,1,0:T(8,128)(2,1)}), bf16[8,128,512]{2,1,0:T(8,128)(2,1)S(1)}, u32[]{:S(2)}, u32[]{:S(2)}) async-start(bf16[8,128,512]{2,1,0:T(8,128)(2,1)} %bitcast.13), calls=%async_computation.2 | async-start | bytes 2097152 | tf_op jit(solution)/shard_map/all_to_all | solution.py:72
Sparse Core Ops, SparseCore 0:
  8.9 60.9 all-gather.1
where the time goes:
time: 205 us
  waiting for transfers between devices  119 us (58%)
  matrix products  23.5 us (11%)
  starting transfers between devices  18.5 us (9%)
  between operations  13.5 us (7%)
  blocking collectives  13.2 us (6%)
  local copies, waits for them, and re-layouts  12.7 us (6%)
  other arithmetic  4.75 us (2%)
    all_to_all x1, waiting for transfers between devices, body(): lax.all_to_all(send_rows, 'wide', split_axis=0, concat_axis=0, tiled=True)  92.8 us
    all_to_all x1, waiting for transfers between devices, body(): lax.all_to_all(adapter_correction, 'wide', split_axis=0, concat_axis=0, t...  25.2 us
    psum x1, blocking collectives, body(): summed = lax.psum(partial_value, 'tensor')  13.2 us
    dot_general x1, matrix products, body(): jnp.dot(gathered, key_value_weight, preferred_element_type=jnp.float32)  11 us
    dot_general x1, matrix products, body(): jnp.dot(flat_rows, down_matrix, preferred_element_type=jnp.float32)  9.95 us
    scatter x1, local copies, waits for them, and re-layouts, body(): send_rows = jnp.zeros((wide_count * capacity, feature_portion), jnp.bfloa...  7.51 us
    all_to_all x1, starting transfers between devices, body(): lax.all_to_all(send_slots, 'wide', split_axis=0, concat_axis=0, tiled=True)  7.25 us
    all_to_all x1, starting transfers between devices, body(): lax.all_to_all(send_rows, 'wide', split_axis=0, concat_axis=0, tiled=True)  5.95 us
  transfers between devices with their start and end apart: 4, of which 2 were waited for; matrix products, arithmetic and copies ran while one was open for 15% of the time, Pallas kernels for 0%

commit v1 on v0

v1 whole, which is shorter than its diff:
```python
import functools

import jax
import jax.numpy as jnp
from jax import lax
from jax.experimental import pallas as pl
from jax.experimental.pallas import tpu as pltpu
from jax.sharding import PartitionSpec as P

MESH = pl.DeviceIdType.MESH
F32 = jnp.float32
BF16 = jnp.bfloat16
LANES = 128


def flip(index, mask, count):
    out, bit = 0, 1
    while bit < count:
        out = out + ((index // bit + mask // bit) % 2) * bit
        bit *= 2
    return out


def iota(shape, dim):
    return lax.broadcasted_iota(jnp.int32, shape, dim)


def to_column(row, size):
    eye = iota((size, row.shape[1]), 0) == iota((size, row.shape[1]), 1)
    return jnp.sum(jnp.where(eye, row, 0.0), axis=1, keepdims=True)


def kernel(
    W,
    T,
    cap,
    per_owner,
    rank,
    tok,
    w_hbm,
    dn_hbm,
    up_hbm,
    apr,
    table,
    out,
    w,
    dn,
    up,
    gat,
    acc,
    rows_out,
    rows_in,
    loc_out,
    loc_in,
    part_out,
    part_in,
    delta_out,
    delta_in,
    load_sem,
    gat_s,
    gat_r,
    row_s,
    row_r,
    loc_s,
    loc_r,
    part_s,
    part_r,
    delta_s,
    delta_r,
):
    me = lax.axis_index("wide")
    te = lax.axis_index("tensor")
    R, F = tok.shape
    C = out.shape[1]
    A = table.shape[1]

    def wide_peer(k):
        return (flip(me, k, W), te)

    def tensor_peer(j):
        return (me, flip(te, j, T))

    barrier = pltpu.get_barrier_semaphore()

    def greet_wide(k, c):
        pl.semaphore_signal(barrier, inc=1, device_id=wide_peer(k), device_id_type=MESH)
        return c

    def greet_tensor(j, c):
        pl.semaphore_signal(barrier, inc=1, device_id=tensor_peer(j), device_id_type=MESH)
        return c

    lax.fori_loop(1, W, greet_wide, 0)
    lax.fori_loop(1, T, greet_tensor, 0)

    load_dn = pltpu.make_async_copy(dn_hbm, dn, load_sem.at[0])
    load_w = pltpu.make_async_copy(w_hbm, w, load_sem.at[1])
    load_up = pltpu.make_async_copy(up_hbm, up, load_sem.at[2])
    load_dn.start()
    load_w.start()
    load_up.start()

    entry = to_column(table[...].astype(F32), A)
    position = jnp.sum(jnp.where(iota((A, R), 0) == apr[...], entry, 0.0), axis=0, keepdims=True)
    owners = max(W, 16)
    owner_id = iota((owners, R), 0).astype(F32)
    hot = jnp.where(
        (position >= owner_id * per_owner) & (position < (owner_id + 1.0) * per_owner), 1.0, 0.0
    )
    before = jnp.where(iota((R, R), 0) < iota((R, R), 1), 1.0, 0.0).astype(BF16)
    earlier = jnp.dot(hot.astype(BF16), before, preferred_element_type=F32)
    owner = jnp.sum(hot * owner_id, axis=0, keepdims=True)
    slot = jnp.sum(hot * earlier, axis=0, keepdims=True) + owner * cap
    local = jnp.broadcast_to(position - owner * per_owner, (16, R)).astype(BF16)
    slot_column = to_column(slot, R)

    pl.semaphore_wait(barrier, W + T - 2)

    def gather(j, src, dst, peer):
        return pltpu.make_async_remote_copy(
            src_ref=src,
            dst_ref=gat.at[dst],
            send_sem=gat_s.at[j],
            recv_sem=gat_r.at[dst],
            device_id=tensor_peer(peer),
            device_id_type=MESH,
        )

    for j in range(2, T, 2):
        gather(j, tok, j, j).start()
    gather(1, tok, 1, 1).start()

    def row_copy(k):
        return pltpu.make_async_remote_copy(
            src_ref=rows_out.at[k],
            dst_ref=rows_in.at[k],
            send_sem=row_s.at[k],
            recv_sem=row_r.at[k],
            device_id=wide_peer(k),
            device_id_type=MESH,
        )

    def loc_copy(k):
        return pltpu.make_async_remote_copy(
            src_ref=loc_out.at[k],
            dst_ref=loc_in.at[k],
            send_sem=loc_s.at[k],
            recv_sem=loc_r.at[k],
            device_id=wide_peer(k),
            device_id_type=MESH,
        )

    def part_copy(k, j):
        return pltpu.make_async_remote_copy(
            src_ref=part_out.at[k],
            dst_ref=part_in.at[k, j],
            send_sem=part_s.at[k, j],
            recv_sem=part_r.at[k, j],
            device_id=tensor_peer(j),
            device_id_type=MESH,
        )

    def delta_copy(k):
        return pltpu.make_async_remote_copy(
            src_ref=delta_out.at[k],
            dst_ref=delta_in.at[k],
            send_sem=delta_s.at[k],
            recv_sem=delta_r.at[k],
            device_id=wide_peer(k),
            device_id_type=MESH,
        )

    def build(k, rows, loc):
        d = flip(me, k, W)
        size = max(cap, LANES)
        pick = jnp.where(
            (iota((size, R), 0) + d * cap).astype(F32) == slot, 1.0, 0.0
        ).astype(BF16)
        loc[k] = lax.dot_general(
            local, pick, (((1,), (1,)), ((), ())), preferred_element_type=F32
        )[:8, :LANES]
        step = min(512, F)
        for c in range(0, F, step):
            rows[k, :, c : c + step] = jnp.dot(
                pick[:cap], tok[:, c : c + step], preferred_element_type=F32
            ).astype(BF16)

    def send(k, c):
        build(k, rows_out, loc_out)
        loc_copy(k).start()
        row_copy(k).start()
        return c

    lax.fori_loop(W // 2, W, send, 0)
    lax.fori_loop(1, W // 2, send, 0)
    build(0, rows_in, loc_in)

    tile = min(256, C)

    def base(j, src, first):
        start = pl.multiple_of(flip(te, j, T) * F, F)

        def columns(n, c):
            cols = pl.ds(pl.multiple_of(n * tile, tile), tile)
            value = jnp.dot(src[...], w[pl.ds(start, F), cols], preferred_element_type=F32)
            if first:
                acc[:, cols] = value
            else:
                acc[:, cols] += value
            return c

        lax.fori_loop(0, C // tile, columns, 0)

    half = cap // 2
    lane = iota((cap, LANES), 1)
    upper = (lane >= rank).astype(F32)
    pairs = per_owner * rank // LANES

    def place(k):
        column = to_column(loc_in[k][:1, :], cap)
        pair = jnp.floor(column * 0.5)
        own = jnp.broadcast_to(column - 2.0 * pair, (cap, LANES)) == upper
        return pair, own

    def shrink(k, c):
        pair, own = place(k)
        total = jnp.zeros((cap, LANES), F32)
        for a in range(0, pairs, 2):
            value = jnp.dot(
                rows_in[k], dn[:, a * LANES : (a + 2) * LANES], preferred_element_type=F32
            )
            total += jnp.where(pair == a, value[:, :LANES], 0.0)
            total += jnp.where(pair == a + 1, value[:, LANES:], 0.0)
        total = jnp.where(own, total, 0.0)
        total += pltpu.roll(total, rank, 1)
        part_out[k] = jnp.where(lane[:half] < rank, total[:half], total[half:])

        def start(j, c):
            part_copy(k, j).start()
            return c

        return lax.fori_loop(1, T, start, c)

    def expand(k):
        def add(j, total):
            part_copy(k, j).wait_recv()
            return total + part_in[k, j]

        total = lax.fori_loop(1, T, add, part_out[k])
        other = pltpu.roll(total, rank, 1)
        low = lane[:half] < rank
        both = jnp.concatenate(
            [jnp.where(low, total, other), jnp.where(low, other, total)], axis=0
        )
        pair, own = place(k)
        both = jnp.where(own, both, 0.0)
        wide = jnp.concatenate(
            [jnp.where(pair == a, both, 0.0).astype(BF16) for a in range(pairs)], axis=1
        )
        return jnp.dot(wide, up[...], preferred_element_type=F32).astype(BF16)

    def arrive(k, c):
        loc_copy(k).wait_recv()
        row_copy(k).wait_recv()
        return shrink(k, c)

    def reply(k, c):
        delta_out[k] = expand(k)
        delta_copy(k).start()
        return c

    def add_delta(k, c):
        d = flip(me, k, W)
        pick = jnp.where(
            (iota((R, cap), 1) + d * cap).astype(F32) == slot_column, 1.0, 0.0
        ).astype(BF16)
        acc[...] += jnp.dot(pick, delta_in[k], preferred_element_type=F32)
        return c

    load_w.wait()
    base(0, tok, True)
    load_dn.wait()
    load_up.wait()
    shrink(0, 0)
    gather(1, tok, 1, 1).wait_recv()
    base(1, gat.at[1], False)
    delta_in[0] = expand(0)
    add_delta(0, 0)

    lax.fori_loop(1, W // 2, arrive, 0)
    for j in range(2, T, 2):
        gather(j, tok, j, j).wait_recv()
        gather(j + 1, gat.at[j], j + 1, 1).start()
        base(j, gat.at[j], False)
    lax.fori_loop(1, W // 2, reply, 0)
    for j in range(2, T, 2):
        gather(j + 1, gat.at[j], j + 1, 1).wait_recv()
        base(j + 1, gat.at[j + 1], False)

    lax.fori_loop(W // 2, W, arrive, 0)
    lax.fori_loop(W // 2, W, reply, 0)

    def collect(k, c):
        delta_copy(k).wait_recv()
        return add_delta(k, c)

    lax.fori_loop(1, W, collect, 0)
    out[...] = acc[...].astype(BF16)

    def drain(k, c):
        loc_copy(k).wait_send()
        row_copy(k).wait_send()
        delta_copy(k).wait_send()
        return c

    lax.fori_loop(1, W, drain, 0)

    def drain_part(k, c):
        def one(j, c):
            part_copy(k, j).wait_send()
            return c

        return lax.fori_loop(1, T, one, c)

    lax.fori_loop(0, W, drain_part, 0)
    gather(1, tok, 1, 1).wait_send()
    for j in range(2, T, 2):
        gather(j, tok, j, j).wait_send()
        gather(j + 1, gat.at[j], j + 1, 1).wait_send()


def body(tokens, weight, down, up, adapter_per_row, table):
    R, F = tokens.shape
    W = lax.axis_size("wide")
    T = lax.axis_size("tensor")
    cap = 2 * R // W
    per_owner, rank = down.shape[1:]
    D, C = weight.shape
    N = per_owner * rank
    vmem = pl.BlockSpec(memory_space=pltpu.VMEM)
    hbm = pl.BlockSpec(memory_space=pl.ANY)
    dma = pltpu.SemaphoreType.DMA
    return pl.pallas_call(
        functools.partial(kernel, W, T, cap, per_owner, rank),
        out_shape=jax.ShapeDtypeStruct((R, C), BF16),
        in_specs=[vmem, hbm, hbm, hbm, vmem, vmem],
        out_specs=vmem,
        scratch_shapes=[
            pltpu.VMEM((D, C), BF16),
            pltpu.VMEM((F, N), BF16),
            pltpu.VMEM((N, C), BF16),
            pltpu.VMEM((T, R, F), BF16),
            pltpu.VMEM((R, C), F32),
            pltpu.VMEM((W, cap, F), BF16),
            pltpu.VMEM((W, cap, F), BF16),
            pltpu.VMEM((W, 8, LANES), F32),
            pltpu.VMEM((W, 8, LANES), F32),
            pltpu.VMEM((W, cap // 2, LANES), F32),
            pltpu.VMEM((W, T, cap // 2, LANES), F32),
            pltpu.VMEM((W, cap, C), BF16),
            pltpu.VMEM((W, cap, C), BF16),
            dma((3,)),
            dma((T,)),
            dma((T,)),
            dma((W,)),
            dma((W,)),
            dma((W,)),
            dma((W,)),
            dma((W, T)),
            dma((W, T)),
            dma((W,)),
            dma((W,)),
        ],
        compiler_params=pltpu.CompilerParams(
            collective_id=0, has_side_effects=True, vmem_limit_bytes=56 * 1024 * 1024
        ),
    )(
        tokens,
        weight,
        down.reshape(F, N),
        up.reshape(N, C),
        adapter_per_row.reshape(1, R),
        table.reshape(1, table.shape[0]),
    )


def solution(mesh):
    in_specs = (
        P("wide", "tensor"),
        P(None, "tensor"),
        P("tensor", "wide", None),
        P("wide", None, "tensor"),
        P("wide"),
        P(),
    )
    out_specs = P("wide", "tensor")
    return jax.shard_map(body, mesh=mesh, in_specs=in_specs, out_specs=out_specs, check_vma=False)
```

time: 205 us -> 135 us (0.66)
  Pallas kernels: 0 us -> 125 us
  waiting for transfers between devices: 119 us -> 0 us
  matrix products: 23.5 us -> 0 us
  starting transfers between devices: 18.5 us -> 0 us
  between operations: 13.5 us -> 0.01 us
  blocking collectives: 13.2 us -> 0 us
  other arithmetic: 4.75 us -> 0 us
  local copies, waits for them, and re-layouts: 12.7 us -> 8.27 us
    pallas_call x0 -> x1, Pallas kernels: none -> 125 us  [body(): pl.pallas_call(functools.partial(kernel, W, T, cap, per_owner, rank), out...]
    all_to_all x3 -> x0, waiting for transfers between devices: 118 us -> none  [the longest x1 92.8 us: body(): lax.all_to_all(send_rows, 'wide', split_axis=0, concat_axis=0, tiled=True)]
    dot_general x3 -> x0, matrix products: 23.5 us -> none  [the longest x1 11 us: body(): jnp.dot(gathered, key_value_weight, preferred_element_type=jnp.float32)]
    all_to_all x3 -> x0, starting transfers between devices: 18.5 us -> none  [the longest x1 7.25 us: body(): lax.all_to_all(send_slots, 'wide', split_axis=0, concat_axis=0, tiled=True)]
    psum x1 -> x0, blocking collectives: 13.2 us -> none  [body(): summed = lax.psum(partial_value, 'tensor')]
    scatter x2 -> x0, local copies, waits for them, and re-layouts: 10.5 us -> none  [the longest x1 7.51 us: body(): send_rows = jnp.zeros((wide_count * capacity, feature_portion), jnp.bfloa...]
    reshape x0 -> x1, local copies, waits for them, and re-layouts: none -> 6.4 us  [body(): down.reshape(F, N)]
    reduce_sum x3 -> x0, other arithmetic: 3.5 us -> none  [the longest x1 2.48 us: body(): jnp.sum(jnp.where(selected, all_ranks, 0.0).reshape(source_rows * entry_l...]
  transfers between devices with their start and end apart: 4 -> 0, of which waited for: 2 -> 0; matrix products, arithmetic and copies ran while one was open for 15% -> 0% of each run, Pallas kernels for 0% -> 0%
where the time goes in v1:
time: 135 us; the launch traced here: 133 us
  Pallas kernels  125 us (93%)
  local copies, waits for them, and re-layouts  8.27 us (6%)
    pallas_call x1, Pallas kernels, body(): pl.pallas_call(functools.partial(kernel, W, T, cap, per_owner, rank), out...  125 us
    reshape x1, local copies, waits for them, and re-layouts, body(): down.reshape(F, N)  6.4 us

profile of v1, /device:TPU:0, one launch (start us, length us, event | category | flops | bytes accessed | tf_op | source)
XLA Modules:
  0.0 133.3 jit_solution(14205234149440393355)
XLA Ops:
  0.0 6.4 %copy.8.dn_hbm = bf16[2048,1024]{1,0:T(8,128)(2,1)} copy(bf16[2048,1024]{0,1:T(8,128)(2,1)} %bitcast.4) | data formatting | bytes 8388608 | tf_op jit(solution)/shard_map/reshape | solution.py:380
  6.4 125.0 %shard_map.64 = bf16[512,512]{1,0:T(8,128)(2,1)} custom-call(bf16[512,2048]{1,0:T(8,128)(2,1)} %tok.1, bf16[8192,512]{1,0:T(8,128)(2,1)} %w_hbm.1, bf16[2048,1024]{1,0:T(8,128)(2,1)} %copy.8.dn_hbm, bf16[1024,512]{1,0:T(8,128)(2,1)} %bitcast.5, s32[1,512]{1,0:T(1,128)} %bitcast.6, s32[1,128]{1,0:T(1,128)} %bitcast.7), custom_call_target="tpu_custom_call" | custom-call | tf_op jit(solution)/shard_map/pallas_call | solution.py:343
  131.4 1.9 %copy.10 = bf16[512,512]{1,0:T(8,128)(2,1)} copy(bf16[512,512]{1,0:T(8,128)(2,1)} %shard_map.64) | data formatting | bytes 1048576

commit v2 on v1

--- a/solution.py
+++ b/solution.py
@@ -226,8 +226,11 @@
         pair, own = place(k)
         total = jnp.zeros((cap, LANES), F32)
         for a in range(0, pairs, 2):
-            value = jnp.dot(
-                rows_in[k], dn[:, a * LANES : (a + 2) * LANES], preferred_element_type=F32
+            value = lax.dot_general(
+                rows_in[k],
+                dn[a * LANES : (a + 2) * LANES],
+                (((1,), (1,)), ((), ())),
+                preferred_element_type=F32,
             )
             total += jnp.where(pair == a, value[:, :LANES], 0.0)
             total += jnp.where(pair == a + 1, value[:, LANES:], 0.0)
@@ -297,8 +300,13 @@
         gather(j + 1, gat.at[j], j + 1, 1).wait_recv()
         base(j + 1, gat.at[j + 1], False)
 
-    lax.fori_loop(W // 2, W, arrive, 0)
-    lax.fori_loop(W // 2, W, reply, 0)
+    def arrive_and_reply(k, c):
+        arrive(k, c)
+        return reply(k - 1, c)
+
+    arrive(W // 2, 0)
+    lax.fori_loop(W // 2 + 1, W, arrive_and_reply, 0)
+    reply(W - 1, 0)
 
     def collect(k, c):
         delta_copy(k).wait_recv()
@@ -347,7 +355,7 @@
         out_specs=vmem,
         scratch_shapes=[
             pltpu.VMEM((D, C), BF16),
-            pltpu.VMEM((F, N), BF16),
+            pltpu.VMEM((N, F), BF16),
             pltpu.VMEM((N, C), BF16),
             pltpu.VMEM((T, R, F), BF16),
             pltpu.VMEM((R, C), F32),
@@ -377,7 +385,7 @@
     )(
         tokens,
         weight,
-        down.reshape(F, N),
+        down.transpose(1, 2, 0).reshape(N, F),
         up.reshape(N, C),
         adapter_per_row.reshape(1, R),
         table.reshape(1, table.shape[0]),

time: 135 us -> 126 us (0.933)
  local copies, waits for them, and re-layouts: 8.27 us -> 1.87 us
  Pallas kernels: 125 us -> 122 us
    reshape x1 -> x0, local copies, waits for them, and re-layouts: 6.4 us -> none  [body(): down.reshape(F, N)]
    pallas_call x1, Pallas kernels: 125 us -> 122 us  [body(): pl.pallas_call(functools.partial(kernel, W, T, cap, per_owner, rank), out...]
where the time goes in v2:
time: 126 us; the launch traced here: 124 us
  Pallas kernels  122 us (97%)
  local copies, waits for them, and re-layouts  1.87 us (1%)
    pallas_call x1, Pallas kernels, body(): pl.pallas_call(functools.partial(kernel, W, T, cap, per_owner, rank), out...  122 us

profile of v2, /device:TPU:0, one launch (start us, length us, event | category | flops | bytes accessed | tf_op | source)
XLA Modules:
  0.0 124.1 jit_solution(5607650582658702049)
XLA Ops:
  0.0 122.2 %shard_map.64 = bf16[512,512]{1,0:T(8,128)(2,1)} custom-call(bf16[512,2048]{1,0:T(8,128)(2,1)} %tok.1, bf16[8192,512]{1,0:T(8,128)(2,1)} %w_hbm.1, bf16[1024,2048]{1,0:T(8,128)(2,1)} %bitcast.6, bf16[1024,512]{1,0:T(8,128)(2,1)} %bitcast.7, s32[1,512]{1,0:T(1,128)} %bitcast.8, s32[1,128]{1,0:T(1,128)} %bitcast.9), custom_call_target="tpu_custom_call" | custom-call | tf_op jit(solution)/shard_map/pallas_call | solution.py:351
  122.2 1.9 %copy.8 = bf16[512,512]{1,0:T(8,128)(2,1)} copy(bf16[512,512]{1,0:T(8,128)(2,1)} %shard_map.64) | data formatting | bytes 1048576
